TPU v7x, 32 devices: a whole 2x2x4 slice. The times are simulated.
32 devices in a mesh: ma: 8 (over z, x), band: 4 (over y, core).
Axes of the slice: x: 2, y: 2, z: 4, core: 2. Of those that a mesh axis runs over, the one named last changes fastest.
Arguments:
- harmonics: bfloat16 [32, 8192, 256], P(('ma', 'band')), may hold values from -6 to 6
- legendre: bfloat16 [32, 2, 8192, 128], P(('ma', 'band')), may hold values from -0.005859375 to 0.005859375
- m_values: int32 [32], replicated, may hold values from 1 to 8191
- cycle_cell: int32 [4096], P(('ma', 'band')), may hold values from 0 to 31, as said below
- phi_cell: int32 [4096], P(('ma', 'band')), may hold values from 3 to 123
- offsets: float32 [2, 4096], P(None, ('ma', 'band')), may hold values from 0 to 1
Outputs:
- lensed: float32 [4096, 128], P(('ma', 'band'))
Inputs may be any that keep to these rules, and one draw needn't show every extreme that they name: `cycle_cell`: Band-local cycle; every point held by device (ma, band) lies in latitude band `band`. For each device and each ma index q, at most 16 of its points have cycles q * 4 to q * 4 + 3, and in every band one q receives exactly 16 points from every device of the band.
All inputs are finite; a program needn't handle non-finite values.
Results may differ from a plain program's by a relative error of at most 0.0053.
Values may be sent and summed in bfloat16 or wider, within the bound.
A program may use at most 64 MiB of HBM per device.

v0:
```python
import jax
import jax.numpy as jnp
from jax import lax
from jax.sharding import PartitionSpec as P

NPHI = 128


def with_halo(x, sides, width):
    for axis, dim in sides:
        count, length = (lax.axis_size(axis), x.shape[dim])
        up = [(i, (i + 1) % count) for i in range(count - 1)]
        down = [(j, i) for i, j in up]
        last = lax.slice_in_dim(x, length - width, length, axis=dim)
        first = lax.slice_in_dim(x, 0, width, axis=dim)
        before = lax.ppermute(last, axis, up)
        after = lax.ppermute(first, axis, down)
        x = jnp.concatenate([before, x, after], axis=dim)
    return x


def kernel_taps(shifts):
    return jnp.sinc(shifts) * jnp.sinc(shifts / 4.0)


def combine_parts(plus_part, minus_part):
    q_real = -(plus_part[:, 0, 0] - minus_part[:, 1, 1])
    q_imag = -(plus_part[:, 0, 1] + minus_part[:, 1, 0])
    u_real = -(plus_part[:, 1, 0] + minus_part[:, 0, 1])
    u_imag = -(plus_part[:, 1, 1] - minus_part[:, 0, 0])
    real_part = jnp.concatenate([q_real, u_real], axis=1)
    imag_part = jnp.concatenate([q_imag, u_imag], axis=1)
    return jnp.stack([real_part, imag_part], axis=1).astype(jnp.bfloat16)


def phase_table(m_values, cell_count, lmax_width):
    pixel_index = jnp.arange(cell_count, dtype=jnp.int32)
    period = 2 * lmax_width
    phase_turns = m_values[None, :] * pixel_index[:, None] % period
    angles = phase_turns.astype(jnp.float32) * (2.0 * jnp.pi / period)
    return jnp.stack([jnp.cos(angles), -jnp.sin(angles)], axis=-1).astype(jnp.bfloat16)


def spectral_cycles(phase_rows, spectra):
    summed = jnp.einsum("kmi,mric->rkc", phase_rows, spectra, preferred_element_type=jnp.float32)
    return (2.0 * summed).astype(jnp.bfloat16)


def spread_weights(starts, weights, length):
    tap_index = jnp.arange(8, dtype=jnp.int32)
    target = starts[:, None] + tap_index[None, :]
    cells = jnp.arange(length, dtype=jnp.int32)
    hits = (target[:, :, None] == cells[None, None, :]).astype(jnp.float32)
    return jnp.sum(weights[:, :, None] * hits, axis=1)


def on_device(harmonics, legendre, m_values, cycle_cell, phi_cell, offsets):
    evolutions = harmonics.shape[2] // 4
    cycle_total = legendre.shape[3]
    contract = (((0,), (0,)), ((), ()))
    plus_part = lax.dot_general(
        legendre[0, 0], harmonics[0], contract, preferred_element_type=jnp.float32
    )
    minus_part = lax.dot_general(
        legendre[0, 1], harmonics[0], contract, preferred_element_type=jnp.float32
    )
    spectra = combine_parts(
        plus_part.reshape(cycle_total, 2, 2, evolutions),
        minus_part.reshape(cycle_total, 2, 2, evolutions),
    )
    width_out = spectra.shape[2]
    owner_count = lax.axis_size("ma")
    band_count = lax.axis_size("band")
    cycle_depth = cycle_total // (owner_count * band_count)
    received = lax.all_to_all(
        spectra[None], ("ma", "band"), split_axis=1, concat_axis=0, tiled=True
    )
    phase_rows = phase_table(m_values, NPHI, harmonics.shape[1])
    wider_spectra = with_halo(received, (("ma", 1),), 4)
    extended = spectral_cycles(phase_rows, wider_spectra)
    ext_rows = extended.shape[0]
    flat_grid = extended.reshape(ext_rows * NPHI, width_out)
    first_cycle = lax.axis_index("ma") * cycle_depth
    capacity = cycle_cell.shape[0] // 8
    owner_index = cycle_cell // cycle_depth
    one_hot = (owner_index[:, None] == jnp.arange(owner_count, dtype=jnp.int32)[None, :]).astype(
        jnp.int32
    )
    slot_index = jnp.sum((jnp.cumsum(one_hot, axis=0) - one_hot) * one_hot, axis=1)
    flat_slot = owner_index * capacity + slot_index
    placement = (
        flat_slot[:, None] == jnp.arange(owner_count * capacity, dtype=jnp.int32)[None, :]
    ).astype(jnp.float32)
    point_table = jnp.stack(
        [cycle_cell.astype(jnp.float32), phi_cell.astype(jnp.float32), offsets[0], offsets[1]],
        axis=1,
    )
    buffers = jnp.dot(placement.T, point_table, precision=lax.Precision.HIGHEST).reshape(
        owner_count, capacity, 4
    )
    cycle_buffer = buffers[:, :, 0].astype(jnp.int32)
    phi_buffer = buffers[:, :, 1].astype(jnp.int32)
    offset_buffer = buffers[:, :, 2:4]
    cycles_here = lax.all_to_all(cycle_buffer, "ma", split_axis=0, concat_axis=0, tiled=True)
    phis_here = lax.all_to_all(phi_buffer, "ma", split_axis=0, concat_axis=0, tiled=True)
    offsets_here = lax.all_to_all(offset_buffer, "ma", split_axis=0, concat_axis=0, tiled=True)
    sources, items = cycles_here.shape
    cycles_flat = cycles_here.reshape(-1)
    phis_flat = phis_here.reshape(-1)
    pairs = offsets_here.reshape(-1, 2)
    tap_shift = jnp.arange(8).astype(jnp.float32) - 3.0
    across = kernel_taps(tap_shift[None, :] - pairs[:, 0:1])
    beside_all = kernel_taps(tap_shift[None, :] - pairs[:, 1:2])
    cycle_weights = spread_weights(cycles_flat + 1 - first_cycle, across, ext_rows)
    phi_weights = spread_weights(phis_flat - 3, beside_all, NPHI)
    dense = (cycle_weights[:, :, None] * phi_weights[:, None, :]).astype(jnp.bfloat16)
    dense = dense.reshape(cycles_flat.shape[0], ext_rows * NPHI)
    values = jnp.dot(dense, flat_grid, preferred_element_type=jnp.float32)
    values = values.reshape(sources, items, width_out)
    returned = lax.all_to_all(values, "ma", split_axis=0, concat_axis=0, tiled=True)
    return jnp.dot(
        placement,
        returned.reshape(owner_count * capacity, width_out),
        precision=lax.Precision.HIGHEST,
    )


def solution(mesh):
    in_specs = (
        P(("ma", "band"), None, None),
        P(("ma", "band"), None, None, None),
        P(),
        P(("ma", "band")),
        P(("ma", "band")),
        P(None, ("ma", "band")),
    )
    out_specs = P(("ma", "band"), None)
    return jax.shard_map(
        on_device, mesh=mesh, in_specs=in_specs, out_specs=out_specs, check_vma=False
    )
```

profile of v0, /device:TPU:0, one launch (start us, length us, event | category | flops | bytes accessed | tf_op | source)
XLA Modules:
  0.0 77.4 jit_solution(1151742660551415633)
XLA Ops:
  0.0 0.7 convert_bitcast_fusion.1
  0.7 0.1 fusion.15
  0.8 0.2 reduce_window_sum.11
  1.0 0.2 select_reduce_fusion.1
  1.2 0.8 slice_bitcast_fusion.3
  2.0 0.7 convert_bitcast_fusion
  2.6 0.2 fusion.14
  2.8 0.1 reshape.275
  2.9 0.6 slice_convert_fusion.1
  3.5 7.3 %all-to-all-start = ((s32[8,1,16]{2,1,0:T(1,128)}), s32[8,1,16]{2,1,0:T(1,128)S(1)}, u32[]{:S(2)}, u32[]{:S(2)}) async-start(s32[8,1,16]{2,1,0:T(1,128)} %bitcast.5), calls=%async_computation | async-start | bytes 8192 | tf_op jit(solution)/shard_map/all_to_all | solution.py:104
  10.8 6.4 %copy.54 = bf16[1,8192,256]{1,2,0:T(8,128)(2,1)} copy(bf16[1,8192,256]{2,1,0:T(8,128)(2,1)} %param.7) | data formatting | bytes 8388608 | tf_op args[0]
  17.2 0.0 copy-start
  17.2 4.2 %fusion = f32[128,2,2,64]{0,3,2,1:T(8,128)S(1)} fusion(bf16[2,2,64,8192]{3,2,1,0:T(8,128)(2,1)} %bitcast.75, bf16[1,2,8192,128]{3,2,1,0:T(8,128)(2,1)} %param.8), kind=kOutput, calls=%fused_computation | convolution fusion | flops 536870912 | bytes 6422528 | tf_op jit(solution)/shard_map/dot_general | solution.py:64
  21.4 0.0 copy-done
  21.4 0.0 copy-start.1
  21.4 2.8 %fusion.2 = f32[128,2,2,64]{0,3,2,1:T(8,128)S(1)} fusion(bf16[2,2,64,8192]{3,2,1,0:T(8,128)(2,1)S(1)} %bitcast.76, bf16[1,2,8192,128]{3,2,1,0:T(8,128)(2,1)} %param.8), kind=kOutput, calls=%fused_computation.2 | convolution fusion | flops 536870912 | bytes 6422528 | tf_op jit(solution)/shard_map/dot_general | solution.py:61
  24.3 0.0 copy-done.1
  24.3 0.2 cosine_convert_fusion
  24.5 0.0 all-to-all-done
  24.5 6.0 %all-to-all-start.2 = ((s32[8,1,16]{2,1,0:T(1,128)}), s32[8,1,16]{2,1,0:T(1,128)S(1)}, u32[]{:S(2)}, u32[]{:S(2)}) async-start(s32[8,1,16]{2,1,0:T(1,128)} %bitcast.8), calls=%async_computation.2 | async-start | bytes 8192 | tf_op jit(solution)/shard_map/all_to_all | solution.py:105
  30.5 0.8 copy.55
  31.3 0.6 copy.49
  31.9 5.1 %all-to-all-done.2 = s32[8,1,16]{2,1,0:T(1,128)S(1)} async-done(((s32[8,1,16]{2,1,0:T(1,128)}), s32[8,1,16]{2,1,0:T(1,128)S(1)}, u32[]{:S(2)}, u32[]{:S(2)}) %all-to-all-start.2) | async-done | bytes 544 | tf_op jit(solution)/shard_map/all_to_all | solution.py:105
  37.0 3.3 %all-to-all-start.1 = ((f32[8,16,2]{1,2,0:T(2,128)}), f32[8,16,2]{1,2,0:T(2,128)S(1)}, u32[]{:S(2)}, u32[]{:S(2)}) async-start(f32[8,16,2]{1,2,0:T(2,128)} %copy.49), calls=%async_computation.1 | async-start | bytes 16384 | tf_op jit(solution)/shard_map/all_to_all | solution.py:106
  40.3 0.1 sub.81
  40.4 0.1 sub.88
  40.4 0.1 iota_add_fusion
  40.6 6.1 %all-to-all-done.1 = f32[8,16,2]{1,2,0:T(2,128)S(1)} async-done(((f32[8,16,2]{1,2,0:T(2,128)}), f32[8,16,2]{1,2,0:T(2,128)S(1)}, u32[]{:S(2)}, u32[]{:S(2)}) %all-to-all-start.1) | async-done | bytes 1056 | tf_op jit(solution)/shard_map/all_to_all | solution.py:106
  46.7 2.6 %all-to-all-start.3 = ((bf16[1,128,2,128]{3,2,0,1:T(2,128)(2,1)}), bf16[1,128,2,128]{3,2,0,1:T(2,128)(2,1)S(1)}, u32[]{:S(2)}, u32[]{:S(2)}) async-start(bf16[1,128,2,128]{3,2,0,1:T(2,128)(2,1)} %copy.55), calls=%async_computation.3 | async-start | bytes 131072 | tf_op jit(solution)/shard_map/all_to_all | solution.py:75
  49.3 0.1 reshape.276
  49.4 0.1 fusion.62
  49.5 0.1 copy.51
  49.6 0.1 copy.53
  49.7 0.3 select_reduce_fusion
  50.1 6.6 %all-to-all-done.3 = bf16[1,128,2,128]{3,2,0,1:T(2,128)(2,1)S(1)} async-done(((bf16[1,128,2,128]{3,2,0,1:T(2,128)(2,1)}), bf16[1,128,2,128]{3,2,0,1:T(2,128)(2,1)S(1)}, u32[]{:S(2)}, u32[]{:S(2)}) %all-to-all-start.3) | async-done | bytes 65568 | tf_op jit(solution)/shard_map/all_to_all | solution.py:75
  56.7 2.5 %collective-permute-start = (bf16[32,4,2,128]{3,0,2,1:T(8,128)(2,1)S(1)}, bf16[32,4,2,128]{3,0,2,1:T(8,128)(2,1)S(1)}, u32[]{:S(2)}, u32[]{:S(2)}) collective-permute-start(bf16[32,4,2,128]{3,0,2,1:T(8,128)(2,1)S(1)} %copy.57), channel_id=1, source_target_pairs={{0,4},{4,8},{8,12},{12,16},{16,20},{20,24},{24,28},{1,5},{5,9},{9,... | collective-permute-start | bytes 196616 | tf_op jit(solution)/shard_map/ppermute | solution.py:16
  59.3 1.3 %collective-permute-start.1 = (bf16[32,4,2,128]{3,0,2,1:T(8,128)(2,1)S(1)}, bf16[32,4,2,128]{3,0,2,1:T(8,128)(2,1)S(1)}, u32[]{:S(2)}, u32[]{:S(2)}) collective-permute-start(bf16[32,4,2,128]{3,0,2,1:T(8,128)(2,1)S(1)} %copy.57), channel_id=1, source_target_pairs={{4,0},{8,4},{12,8},{16,12},{20,16},{24,20},{28,24},{5,1},{9,5},{13... | collective-permute-start | bytes 196616 | tf_op jit(solution)/shard_map/ppermute | solution.py:17
  60.6 0.3 multiply_convert_fusion
  60.9 0.3 convert_element_type.102
  61.2 0.0 collective-permute-done
  61.2 4.2 %collective-permute-done.1 = bf16[32,4,2,128]{3,0,2,1:T(8,128)(2,1)S(1)} collective-permute-done((bf16[32,4,2,128]{3,0,2,1:T(8,128)(2,1)S(1)}, bf16[32,4,2,128]{3,0,2,1:T(8,128)(2,1)S(1)}, u32[]{:S(2)}, u32[]{:S(2)}) %collective-permute-start.1) | collective-permute-done | bytes 65568 | tf_op jit(solution)/shard_map/ppermute | solution.py:17
  65.4 0.3 fusion.7
  65.7 0.3 fusion.133
  66.0 10.6 %all_to_all.34 = f32[8,16,128]{2,1,0:T(8,128)S(1)} all-to-all(f32[8,16,128]{2,1,0:T(8,128)S(1)} %fusion.133), channel_id=1, replica_groups=mesh['ma'=8,'band'=4] {'ma'}, dimensions={0} | all-to-all | bytes 131072 | tf_op jit(solution)/shard_map/all_to_all | solution.py:120
  76.6 0.9 %fusion.13 = f32[128,128]{1,0:T(8,128)} fusion(f32[128,128]{1,0:T(8,128)S(1)} %bitcast.78, s32[128]{0:T(128)S(1)} %multiply_add_fusion.4), kind=kOutput, calls=%fused_computation.20 | convolution fusion | flops 25182208 | bytes 131584 | tf_op jit(solution)/shard_map/dot_general | solution.py:121
  (13 shorter events, 0.1 us)
Async XLA Ops:
  3.5 21.0 %all-to-all-start = ((s32[8,1,16]{2,1,0:T(1,128)}), s32[8,1,16]{2,1,0:T(1,128)S(1)}, u32[]{:S(2)}, u32[]{:S(2)}) async-start(s32[8,1,16]{2,1,0:T(1,128)} %bitcast.5), calls=%async_computation | async-start | bytes 8192 | tf_op jit(solution)/shard_map/all_to_all | solution.py:104
  17.2 4.2 %copy-start = (bf16[1,8192,256]{1,2,0:T(8,128)(2,1)S(1)}, bf16[1,8192,256]{1,2,0:T(8,128)(2,1)}, u32[]{:S(2)}) copy-start(bf16[1,8192,256]{1,2,0:T(8,128)(2,1)} %copy.54) | copy-start | bytes 12582916
  21.4 2.9 %copy-start.1 = (s32[32]{0:T(128)S(1)}, s32[32]{0:T(128)}, u32[]{:S(2)}) copy-start(s32[32]{0:T(128)} %param.9) | copy-start | bytes 388
  24.5 12.5 %all-to-all-start.2 = ((s32[8,1,16]{2,1,0:T(1,128)}), s32[8,1,16]{2,1,0:T(1,128)S(1)}, u32[]{:S(2)}, u32[]{:S(2)}) async-start(s32[8,1,16]{2,1,0:T(1,128)} %bitcast.8), calls=%async_computation.2 | async-start | bytes 8192 | tf_op jit(solution)/shard_map/all_to_all | solution.py:105
  37.0 9.7 %all-to-all-start.1 = ((f32[8,16,2]{1,2,0:T(2,128)}), f32[8,16,2]{1,2,0:T(2,128)S(1)}, u32[]{:S(2)}, u32[]{:S(2)}) async-start(f32[8,16,2]{1,2,0:T(2,128)} %copy.49), calls=%async_computation.1 | async-start | bytes 16384 | tf_op jit(solution)/shard_map/all_to_all | solution.py:106
  46.7 10.0 %all-to-all-start.3 = ((bf16[1,128,2,128]{3,2,0,1:T(2,128)(2,1)}), bf16[1,128,2,128]{3,2,0,1:T(2,128)(2,1)S(1)}, u32[]{:S(2)}, u32[]{:S(2)}) async-start(bf16[1,128,2,128]{3,2,0,1:T(2,128)(2,1)} %copy.55), calls=%async_computation.3 | async-start | bytes 131072 | tf_op jit(solution)/shard_map/all_to_all | solution.py:75
  56.7 4.4 %collective-permute-start = (bf16[32,4,2,128]{3,0,2,1:T(8,128)(2,1)S(1)}, bf16[32,4,2,128]{3,0,2,1:T(8,128)(2,1)S(1)}, u32[]{:S(2)}, u32[]{:S(2)}) collective-permute-start(bf16[32,4,2,128]{3,0,2,1:T(8,128)(2,1)S(1)} %copy.57), channel_id=1, source_target_pairs={{0,4},{4,8},{8,12},{12,16},{16,20},{20,24},{24,28},{1,5},{5,9},{9,... | collective-permute-start | bytes 196616 | tf_op jit(solution)/shard_map/ppermute | solution.py:16
  59.3 6.2 %collective-permute-start.1 = (bf16[32,4,2,128]{3,0,2,1:T(8,128)(2,1)S(1)}, bf16[32,4,2,128]{3,0,2,1:T(8,128)(2,1)S(1)}, u32[]{:S(2)}, u32[]{:S(2)}) collective-permute-start(bf16[32,4,2,128]{3,0,2,1:T(8,128)(2,1)S(1)} %copy.57), channel_id=1, source_target_pairs={{4,0},{8,4},{12,8},{16,12},{20,16},{24,20},{28,24},{5,1},{9,5},{13... | collective-permute-start | bytes 196616 | tf_op jit(solution)/shard_map/ppermute | solution.py:17
where the time goes:
time: 78 us; the launch traced here: 77.4 us
  starting transfers between devices  22.9 us (29%)
  waiting for transfers between devices  22.1 us (28%)
  blocking collectives  10.6 us (14%)
  local copies, waits for them, and re-layouts  9.34 us (12%)
  matrix products  8.68 us (11%)
  other arithmetic  3.58 us (5%)
    all_to_all x1, blocking collectives, on_device(): lax.all_to_all(values, 'ma', split_axis=0, concat_axis=0, tiled=True)  10.6 us
    all_to_all x1, starting transfers between devices, on_device(): lax.all_to_all(cycle_buffer, 'ma', split_axis=0, concat_axis=0, tiled=True)  7.25 us
    all_to_all x1, waiting for transfers between devices, on_device(): lax.all_to_all(spectra[None], ('ma', 'band'), split_axis=1, concat_axis=0...  6.62 us
    unnamed x5, local copies, waits for them, and re-layouts  6.39 us
    all_to_all x1, waiting for transfers between devices, on_device(): lax.all_to_all(offset_buffer, 'ma', split_axis=0, concat_axis=0, tiled=True)  6.15 us
    all_to_all x1, starting transfers between devices, on_device(): lax.all_to_all(phi_buffer, 'ma', split_axis=0, concat_axis=0, tiled=True)  6 us
    all_to_all x1, waiting for transfers between devices, on_device(): lax.all_to_all(phi_buffer, 'ma', split_axis=0, concat_axis=0, tiled=True)  5.08 us
    ppermute x1, waiting for transfers between devices, with_halo(): after = lax.ppermute(first, axis, down)  4.23 us
  transfers between devices with their start and end apart: 6, of which 4 were waited for; matrix products, arithmetic and copies ran while one was open for 22% of the time, Pallas kernels for 0%

commit v1 on v0

v1 whole, which is shorter than its diff:
```python
import functools

import jax
import jax.numpy as jnp
from jax import lax
from jax.experimental import pallas as pl
from jax.experimental.pallas import tpu as pltpu
from jax.sharding import PartitionSpec as P

NPHI = 128
LANES = 128
TAPS = 8
MESH = pl.DeviceIdType.MESH
F32 = jnp.float32
BF16 = jnp.bfloat16


def sinc(x):
    t = jnp.pi * x
    small = x == 0.0
    return jnp.where(small, 1.0, jnp.sin(t) / jnp.where(small, 1.0, t))


def taps_of(offset_row):
    steps = lax.broadcasted_iota(jnp.int32, (TAPS, offset_row.shape[1]), 0).astype(F32) - 3.0
    shifts = steps - offset_row
    return sinc(shifts) * sinc(shifts / 4.0)


def kernel(
    dims, harm, leg, m_ref, cell_ref, phi_ref, off_ref, out_ref,
    harm_v, leg_v, acc, pts, phase, weights, send, recv, back, ret,
    load_sems, pts_send, pts_recv, spec_send, spec_recv, ret_send, ret_recv,
):
    owners, bands, depth, period, chunk, prebuilt = dims
    total = owners * bands
    length, columns = harm.shape
    cycles = leg.shape[2]
    evolutions = columns // 4
    width = 2 * evolutions
    rows = cycles // bands
    share = width // owners
    pieces = length // chunk
    pack = LANES // (2 * rows)
    ma = lax.axis_index("ma")
    band = lax.axis_index("band")
    me = ma * bands + band

    def loads(step):
        here = pl.ds(pl.multiple_of(step * chunk, chunk), chunk)
        pairs = [(harm.at[here], harm_v.at[here])]
        for half in range(2):
            pairs.append((leg.at[half, here], leg_v.at[here, pl.ds(half * cycles, cycles)]))
        return [
            pltpu.make_async_copy(src, dst, load_sems.at[n, step])
            for n, (src, dst) in enumerate(pairs)
        ]

    def start_loads(step, carry):
        for copy in loads(step):
            copy.start()
        return carry

    lax.fori_loop(0, pieces, start_loads, 0)

    barrier = pltpu.get_barrier_semaphore()

    def greet(step, carry):
        peer = lax.rem(me + step, total)
        pl.semaphore_signal(
            barrier, inc=1, device_id=(peer // bands, lax.rem(peer, bands)), device_id_type=MESH
        )
        return carry

    lax.fori_loop(1, total, greet, 0)

    pts[ma, 0:TAPS, :] = taps_of(off_ref[0:1, :])
    pts[ma, TAPS:2 * TAPS, :] = taps_of(off_ref[1:2, :])
    row = lax.broadcasted_iota(jnp.int32, (TAPS, LANES), 0)
    pts[ma, 2 * TAPS:3 * TAPS, :] = jnp.where(
        row == 0, cell_ref[...], jnp.where(row == 1, phi_ref[...], 0)
    ).astype(F32)

    pl.semaphore_wait(barrier, total - 1)

    def send_points(step, carry):
        peer = lax.rem(ma + step, owners)
        pltpu.make_async_remote_copy(
            src_ref=pts.at[ma], dst_ref=pts.at[ma], send_sem=pts_send, recv_sem=pts_recv,
            device_id=(peer, band), device_id_type=MESH,
        ).start()
        return carry

    lax.fori_loop(1, owners, send_points, 0)

    eye = lax.broadcasted_iota(jnp.int32, (total, total), 0) == lax.broadcasted_iota(
        jnp.int32, (total, total), 1
    )
    m_column = jnp.sum(jnp.where(eye, m_ref[...].astype(F32), 0.0), axis=1, keepdims=True)
    pixel = lax.broadcasted_iota(jnp.int32, (total, NPHI), 1)
    turns = lax.rem(m_column.astype(jnp.int32) * pixel, period)
    angles = turns.astype(F32) * (2.0 * jnp.pi / period)
    phase[0:total, :] = jnp.cos(angles).astype(BF16)
    phase[total:2 * total, :] = (-jnp.sin(angles)).astype(BF16)

    acc[...] = jnp.zeros_like(acc)

    def multiply(step, carry):
        for copy in loads(step):
            copy.wait()
        here = pl.ds(pl.multiple_of(step * chunk, chunk), chunk)
        acc[...] += lax.dot_general(
            harm_v[here, :], leg_v[here, :], (((0,), (0,)), ((), ())),
            preferred_element_type=F32,
        )
        return carry

    lax.fori_loop(0, pieces, multiply, 0)

    def part(half, which):
        return acc[which * evolutions:(which + 1) * evolutions, half * cycles:(half + 1) * cycles]

    q_real = -(part(0, 0) - part(1, 3))
    q_imag = -(part(0, 1) + part(1, 2))
    u_real = -(part(0, 2) + part(1, 1))
    u_imag = -(part(0, 3) - part(1, 0))
    real = jnp.concatenate([q_real, u_real], axis=0)
    imag = jnp.concatenate([q_imag, u_imag], axis=0)
    spectra = jnp.concatenate([real, imag], axis=1).astype(BF16)

    source = lax.broadcasted_iota(jnp.int32, (2 * cycles, LANES), 0)
    lane = lax.broadcasted_iota(jnp.int32, (2 * cycles, LANES), 1)
    inner = lax.rem(lane, 2 * rows)
    j = lax.rem(inner, rows)
    mine = (lane // (2 * rows)) == lax.rem(me, pack)
    for b in range(bands):
        place = (inner // rows) * cycles + ((j // depth) * bands + b) * depth + lax.rem(j, depth)
        pick = jnp.where(mine & (source == place), 1.0, 0.0).astype(BF16)
        send[b] = jnp.dot(spectra, pick, preferred_element_type=F32).astype(send.dtype)

    def send_spectra(step, carry):
        peer = lax.rem(me + step, total)
        to_ma, to_band = peer // bands, lax.rem(peer, bands)
        pltpu.make_async_remote_copy(
            src_ref=send.at[to_band, pl.ds(pl.multiple_of(to_ma * share, share), share)],
            dst_ref=recv.at[me], send_sem=spec_send, recv_sem=spec_recv,
            device_id=(to_ma, to_band), device_id_type=MESH,
        ).start()
        return carry

    lax.fori_loop(1, total, send_spectra, 0)
    recv[me] = send[band, pl.ds(pl.multiple_of(ma * share, share), share), :]

    others = pl.ds(0, owners - 1)
    pltpu.make_async_copy(pts.at[others], pts.at[others], pts_recv).wait()

    def build(s, column):
        pixels = lax.broadcasted_iota(jnp.int32, (NPHI, LANES), 0)
        ring = lax.broadcasted_iota(jnp.int32, (rows, LANES), 0)
        table = pts[s]
        cell = table[2 * TAPS:2 * TAPS + 1].astype(jnp.int32)
        phi = table[2 * TAPS + 1:2 * TAPS + 2].astype(jnp.int32)
        across = jnp.zeros((rows, LANES), F32)
        beside = jnp.zeros((NPHI, LANES), F32)
        for e in range(TAPS):
            across = jnp.where(ring == cell + (e - 3), table[e:e + 1], across)
            beside = jnp.where(pixels == phi + (e - 3), table[TAPS + e:TAPS + e + 1], beside)
        across = 2.0 * across
        high = beside.astype(BF16)
        low = (beside - high.astype(F32)).astype(BF16)
        mixed = jnp.dot(phase[...], high, preferred_element_type=F32) + jnp.dot(
            phase[...], low, preferred_element_type=F32
        )
        for g in range(total):
            for i in range(2):
                at = (g * 2 + i) * rows
                weights[at:at + rows, column] = (
                    mixed[i * total + g:i * total + g + 1] * across
                ).astype(BF16)

    def build_all(s, carry):
        build(s, pl.ds(pl.multiple_of(s * LANES, LANES), LANES))
        return carry

    if prebuilt:
        lax.fori_loop(0, owners, build_all, 0)

    arrived = pl.ds(0, total - 1)
    pltpu.make_async_copy(recv.at[arrived], recv.at[arrived], spec_recv).wait()
    groups = []
    for h in range(total // pack):
        block = recv[h * pack]
        for extra in range(1, pack):
            block = block + recv[h * pack + extra]
        groups.append(block.astype(BF16))
    lined = jnp.concatenate(groups, axis=1)

    for t in range(owners // 2):
        at = 2 * t * LANES if prebuilt else 0
        if not prebuilt:
            for half in range(2):
                build(2 * t + half, pl.ds(half * LANES, LANES))
        values = jnp.dot(lined, weights[:, at:at + 2 * LANES], preferred_element_type=F32)
        for half in range(2):
            s = 2 * t + half
            back[s] = values[:, half * LANES:(half + 1) * LANES]

            @pl.when(s != ma)
            def _():
                pltpu.make_async_remote_copy(
                    src_ref=back.at[s], dst_ref=ret.at[ma], send_sem=ret_send,
                    recv_sem=ret_recv, device_id=(s, band), device_id_type=MESH,
                ).start()

    ret[ma] = back[ma]
    pltpu.make_async_copy(ret.at[others], ret.at[others], ret_recv).wait()
    out_ref[...] = ret[...].reshape(width, LANES).T

    pltpu.make_async_copy(pts.at[others], pts.at[others], pts_send).wait()
    pltpu.make_async_copy(recv.at[arrived], recv.at[arrived], spec_send).wait()
    pltpu.make_async_copy(back.at[others], back.at[others], ret_send).wait()


def on_device(harmonics, legendre, m_values, cycle_cell, phi_cell, offsets):
    owners, bands = lax.axis_size("ma"), lax.axis_size("band")
    total = owners * bands
    _, length, columns = harmonics.shape
    cycles = legendre.shape[3]
    width = columns // 2
    rows = cycles // bands
    share = width // owners
    points = cycle_cell.shape[0]
    depth = cycles // total
    chunk = min(512, length)
    pieces = length // chunk
    contraction = total * 2 * rows
    prebuilt = contraction * owners * points * 2 <= 16 * 2**20
    kept = owners * points if prebuilt else 2 * points
    wire = BF16 if share % 16 == 0 else F32
    dims = (owners, bands, depth, 2 * length, chunk, prebuilt)
    vmem = pl.BlockSpec(memory_space=pltpu.VMEM)
    anywhere = pl.BlockSpec(memory_space=pl.ANY)
    dma = pltpu.SemaphoreType.DMA
    return pl.pallas_call(
        functools.partial(kernel, dims),
        out_shape=jax.ShapeDtypeStruct((points, width), F32),
        in_specs=[anywhere, anywhere, vmem, vmem, vmem, vmem],
        out_specs=vmem,
        scratch_shapes=[
            pltpu.VMEM((length, columns), BF16),
            pltpu.VMEM((length, 2 * cycles), BF16),
            pltpu.VMEM((columns, 2 * cycles), F32),
            pltpu.VMEM((owners, 3 * TAPS, points), F32),
            pltpu.VMEM((2 * total, NPHI), BF16),
            pltpu.VMEM((contraction, kept), BF16),
            pltpu.VMEM((bands, width, LANES), wire),
            pltpu.VMEM((total, share, LANES), wire),
            pltpu.VMEM((owners, share, points), F32),
            pltpu.VMEM((owners, share, points), F32),
            dma((3, pieces)),
            dma, dma, dma, dma, dma, dma,
        ],
        compiler_params=pltpu.CompilerParams(
            collective_id=0, has_side_effects=True, vmem_limit_bytes=56 * 2**20
        ),
    )(
        harmonics[0], legendre[0], m_values.reshape(1, -1), cycle_cell.reshape(1, -1),
        phi_cell.reshape(1, -1), offsets,
    )


def solution(mesh):
    in_specs = (
        P(("ma", "band"), None, None),
        P(("ma", "band"), None, None, None),
        P(),
        P(("ma", "band")),
        P(("ma", "band")),
        P(None, ("ma", "band")),
    )
    out_specs = P(("ma", "band"), None)
    return jax.shard_map(
        on_device, mesh=mesh, in_specs=in_specs, out_specs=out_specs, check_vma=False
    )
```

time: 78 us -> 25.4 us (0.33)
  Pallas kernels: 0 us -> 23.7 us
  starting transfers between devices: 22.9 us -> 0 us
  waiting for transfers between devices: 22.1 us -> 0 us
  blocking collectives: 10.6 us -> 0 us
  matrix products: 8.68 us -> 0 us
  local copies, waits for them, and re-layouts: 9.34 us -> 1.47 us
  other arithmetic: 3.58 us -> 0 us
    pallas_call x0 -> x1, Pallas kernels: none -> 23.7 us  [on_device(): pl.pallas_call(functools.partial(kernel, dims), out_shape=jax.ShapeDtypeS...]
    all_to_all x4 -> x0, starting transfers between devices: 19.1 us -> none  [the longest x1 7.25 us: on_device(): lax.all_to_all(cycle_buffer, 'ma', split_axis=0, concat_axis=0, tiled=True)]
    all_to_all x4 -> x0, waiting for transfers between devices: 17.8 us -> none  [the longest x1 6.62 us: on_device(): lax.all_to_all(spectra[None], ('ma', 'band'), split_axis=1, concat_axis=0...]
    all_to_all x1 -> x0, blocking collectives: 10.6 us -> none  [on_device(): lax.all_to_all(values, 'ma', split_axis=0, concat_axis=0, tiled=True)]
    dot_general x6 -> x0, matrix products: 8.68 us -> none  [the longest x1 4.21 us: on_device(): lax.dot_general(legendre[0, 1], harmonics[0], contract, preferred_element...]
    unnamed x5 -> x1, local copies, waits for them, and re-layouts: 6.39 us -> 1.47 us
    ppermute x2 -> x0, waiting for transfers between devices: 4.23 us -> none  [the longest x1 4.23 us: with_halo(): after = lax.ppermute(first, axis, down)]
    ppermute x2 -> x0, starting transfers between devices: 3.81 us -> none  [the longest x1 2.52 us: with_halo(): before = lax.ppermute(last, axis, up)]
  transfers between devices with their start and end apart: 6 -> 0, of which waited for: 4 -> 0; matrix products, arithmetic and copies ran while one was open for 22% -> 0% of each run, Pallas kernels for 0% -> 0%
where the time goes in v1:
time: 25.4 us; the launch traced here: 25.2 us
  Pallas kernels  23.7 us (93%)
  local copies, waits for them, and re-layouts  1.47 us (6%)
    pallas_call x1, Pallas kernels, on_device(): pl.pallas_call(functools.partial(kernel, dims), out_shape=jax.ShapeDtypeS...  23.7 us
    unnamed x1, local copies, waits for them, and re-layouts  1.47 us

profile of v1, /device:TPU:0, one launch (start us, length us, event | category | flops | bytes accessed | tf_op | source)
XLA Modules:
  0.0 25.2 jit_solution(921044975941895852)
XLA Ops:
  0.0 23.7 %shard_map.64 = f32[128,128]{1,0:T(8,128)} custom-call(bf16[8192,256]{1,0:T(8,128)(2,1)} %bitcast.5, bf16[2,8192,128]{2,1,0:T(8,128)(2,1)} %bitcast.6, s32[1,32]{1,0:T(1,128)} %bitcast.7, s32[1,128]{1,0:T(1,128)} %bitcast.8, s32[1,128]{1,0:T(1,128)} %bitcast.9, f32[2,128]{1,0:T(2,128)} %off_ref.1), custom_call_target="tpu_custom_call" | custom-call | tf_op jit(solution)/shard_map/pallas_call | solution.py:244
  23.7 1.5 %copy.8 = f32[128,128]{1,0:T(8,128)} copy(f32[128,128]{1,0:T(8,128)} %shard_map.64) | data formatting | bytes 131072
